TPU v7x, 128 devices: a whole 4x4x4 slice. The times are simulated.
128 devices in a mesh: ind: 64 (over y, x, z), snp: 2 (over core).
Axes of the slice: x: 4, y: 4, z: 4, core: 2. Of those that a mesh axis runs over, the one named last changes fastest.
Arguments:
- genotypes: bfloat16 [2, 249856, 1024], P(None, 'ind', 'snp'), may hold values from -0.013387887 to 0.013387887
- residual: float32 [32, 249856], P(None, 'ind'), may hold values from -7 to 7
- effects: float32 [2, 32, 1024], P(None, None, 'snp'), may hold values from -6 to 6
- noise: float32 [2, 32, 1024], replicated, may hold values from -6 to 6
- prior_var: float32 [2048], replicated, may hold values from 0.1 to 2
- block_snps: int32 [2048], replicated, may hold values from 0 to 2047, each once
- noise_var: float32 [32], replicated, may hold values from 0.5 to 2
- chi_scaled: float32 [32], replicated, may hold values from 0.8 to 1.25
Outputs:
- new_effects: float32 [2, 32, 1024], P(None, None, 'snp')
- new_residual: float32 [32, 249856], P(None, 'ind')
- variance_draw: float32 [32], replicated
Inputs may be any that keep to these rules, and one draw needn't show every extreme that they name: `block_snps`: every table row appears once; entries b * 1024 to (b + 1) * 1024 - 1 belong to block b.
All inputs are finite; a program needn't handle non-finite values.
Results may differ from a plain program's by a relative error of at most 0.004.
Values may be sent and summed in bfloat16 or wider, within the bound.
No kernel may reach another device: no remote copies, remote signals or barrier semaphores. Data moves between devices by JAX's collectives and lax.ppermute only.
A program may use at most 192 MiB of HBM per device.

v0:
```python
import jax
import jax.numpy as jnp
from jax import lax
from jax.sharding import PartitionSpec as P


def sample_effects(factor, right_side, noise_rows, chain_scale):
    whitened = jax.scipy.linalg.solve_triangular(factor, right_side.T, lower=True)
    moved = whitened + chain_scale * noise_rows.T
    return jax.scipy.linalg.solve_triangular(factor, moved, lower=True, trans=1).T


def local(genotypes, residual, effects, noise, prior_var, block_snps, noise_var, chi_scaled):
    contract_rows = (((0,), (0,)), ((), ()))
    contract_cols = (((1,), (1,)), ((), ()))
    block_count, row_count, half_width = genotypes.shape
    own_offset = lax.axis_index("snp") * half_width
    full_width = half_width * lax.axis_size("snp")
    table_rows = block_snps.reshape(block_count, full_width)
    chain_scale = jnp.sqrt(noise_var)[None, :]
    previous_all = lax.all_gather(effects.astype(jnp.bfloat16), "snp", axis=2, tiled=True).astype(
        effects.dtype
    )
    grams = []
    shifted = []
    for block_index in range(block_count):
        genotype_block = genotypes[block_index]
        partial_gram = lax.dot_general(
            lax.all_gather(genotype_block, "snp", axis=1, tiled=True),
            genotype_block,
            contract_rows,
            preferred_element_type=jnp.float32,
        )
        summed_gram = lax.psum(partial_gram, "ind")
        gram_matrix = lax.all_gather(summed_gram, "snp", axis=1, tiled=True)
        inverse_prior = 1.0 / jnp.take(prior_var, table_rows[block_index])
        grams.append(gram_matrix)
        shifted.append(gram_matrix + jnp.diag(inverse_prior))
    factors = jnp.linalg.cholesky(jnp.stack(shifted))
    sampled_list = []
    for block_index in range(block_count):
        previous = previous_all[block_index]
        gram_matrix = grams[block_index]
        rounded = residual.astype(jnp.bfloat16)
        carried = jnp.dot(previous, gram_matrix, precision=lax.Precision.HIGHEST)
        local_scores = jnp.dot(rounded, genotypes[block_index], preferred_element_type=jnp.float32)
        summed_scores = lax.psum(local_scores, "ind")
        own_half = summed_scores + lax.dynamic_slice_in_dim(carried, own_offset, half_width, 1)
        right_side = lax.all_gather(own_half, "snp", axis=1, tiled=True)
        sampled = sample_effects(factors[block_index], right_side, noise[block_index], chain_scale)
        change = (sampled - previous).astype(jnp.bfloat16)
        own_change = lax.dynamic_slice_in_dim(change, own_offset, half_width, 1)
        partial_update = lax.dot_general(
            own_change, genotypes[block_index], contract_cols, preferred_element_type=jnp.float32
        )
        update = lax.psum(partial_update.astype(jnp.bfloat16), "snp").astype(jnp.float32)
        residual = residual - update
        sampled_list.append(lax.dynamic_slice_in_dim(sampled, own_offset, half_width, 1))
    squares_sum = lax.psum(jnp.sum(residual * residual, axis=1), "ind")
    variance_draw = squares_sum / (row_count * lax.axis_size("ind") * chi_scaled)
    return (jnp.stack(sampled_list), residual, variance_draw)


def solution(mesh):
    placed = (P(None, "ind", "snp"), P(None, "ind"), P(None, None, "snp"), P(), P(), P(), P(), P())
    return jax.shard_map(
        local,
        mesh=mesh,
        in_specs=placed,
        out_specs=(P(None, None, "snp"), P(None, "ind"), P()),
        check_vma=False,
    )
```

profile of v0, /device:TPU:0, one launch (start us, length us, event | category | flops | bytes accessed | tf_op | source)
XLA Modules:
  0.0 1176.8 jit_solution(779579112746427394)
XLA Ops:
  7.2 5.5 fusion.215
  13.8 3.6 fusion.11
  17.4 20.0 %all-gather.11.cloned.1.call-done = bf16[1,3904,1024]{2,1,0:T(8,128)(2,1)} async-done(((bf16[1,3904,512]{2,1,0:T(8,128)(2,1)}), bf16[1,3904,1024]{2,1,0:T(8,128)(2,1)}) %all-gather.11.cloned.1.call-update) | async-done | bytes 7995408 | tf_op jit(solution)/shard_map/all_gather | solution.py:29
  37.4 10.3 fusion.3
  47.6 14.7 %all-gather.13.cloned.1.call-done = bf16[1,3904,1024]{2,1,0:T(8,128)(2,1)} async-done(((bf16[1,3904,512]{2,1,0:T(8,128)(2,1)}), bf16[1,3904,1024]{2,1,0:T(8,128)(2,1)}) %all-gather.13.cloned.1.call-update) | async-done | bytes 7995408 | tf_op jit(solution)/shard_map/all_gather | solution.py:29
  62.4 10.3 fusion.1
  72.7 141.2 %all-reduce.13.cloned.1.call-done = (f32[1024,512]{0,1:T(8,128)}, f32[1024,512]{0,1:T(8,128)}, f32[32,512]{1,0:T(8,128)}) async-done(((f32[1024,512]{0,1:T(8,128)}, f32[1024,512]{0,1:T(8,128)}, f32[32,512]{1,0:T(8,128)}), (f32[1024,512]{0,1:T(8,128)}, f32[1024,512]{0,1:T(8,128)}, f32[32,512]{1,0:T(8,128)})) %all-reduce.13.cloned.1.call-update) | async-done | bytes 4259856 | tf_op jit(solution)/shard_map/psum | solution.py:34
  214.7 6.2 gather_fusion
  220.8 6.2 gather_fusion.1
  230.1 4.5 fusion.96
  236.8 2.4 add_bitcast_fusion.1
  239.1 9.9 all-gather.9.cloned.1.call-done
  249.0 2.7 add_bitcast_fusion
  253.7 4.1 pad_maximum_fusion
  257.8 8.7 copy.47
  266.5 6.9 fusion
  273.4 3.2 copy-done.4
  276.7 23.5 %custom-call.73 = f32[2,128,128]{2,1,0:T(8,128)S(1)} custom-call(f32[2,128,128]{2,1,0:T(8,128)S(1)} %cholesky.578), custom_call_target="Cholesky" | custom-call | tf_op jit(solution)/shard_map/jit(cholesky)/cholesky | solution.py:39
  300.1 19.7 %custom-call.74 = f32[2,1,128,128]{2,3,1,0:T(8,128)S(1)} custom-call(f32[2,1,128,128]{3,2,1,0:T(8,128)S(1)} %select_bitcast_fusion.6), custom_call_target="InvertDiagBlocksLowerTriangular" | custom-call | tf_op jit(solution)/shard_map/jit(cholesky)/cholesky | solution.py:39
  319.8 4.3 cholesky.253
  324.1 3.1 constant_dynamic-update-slice_fusion.107
  329.4 23.9 %custom-call.75 = f32[2,128,128]{2,1,0:T(8,128)S(1)} custom-call(f32[2,128,128]{2,1,0:T(8,128)S(1)} %cholesky.582), custom_call_target="Cholesky" | custom-call | tf_op jit(solution)/shard_map/jit(cholesky)/cholesky | solution.py:39
  353.9 19.7 %custom-call.76 = f32[2,1,128,128]{2,3,1,0:T(8,128)S(1)} custom-call(f32[2,1,128,128]{3,2,1,0:T(8,128)S(1)} %get-tuple-element.88), custom_call_target="InvertDiagBlocksLowerTriangular" | custom-call | tf_op jit(solution)/shard_map/jit(cholesky)/cholesky | solution.py:39
  375.3 3.2 fusion.25
  378.5 23.6 %custom-call.77 = f32[2,128,128]{2,1,0:T(8,128)S(1)} custom-call(f32[2,128,128]{2,1,0:T(8,128)S(1)} %cholesky.587), custom_call_target="Cholesky" | custom-call | tf_op jit(solution)/shard_map/jit(cholesky)/cholesky | solution.py:39
  402.8 19.7 %custom-call.78 = f32[2,1,128,128]{2,3,1,0:T(8,128)S(1)} custom-call(f32[2,1,128,128]{3,2,1,0:T(8,128)S(1)} %get-tuple-element.86), custom_call_target="InvertDiagBlocksLowerTriangular" | custom-call | tf_op jit(solution)/shard_map/jit(cholesky)/cholesky | solution.py:39
  424.1 3.8 fusion.28
  427.9 23.7 %custom-call.79 = f32[2,128,128]{2,1,0:T(8,128)S(1)} custom-call(f32[2,128,128]{2,1,0:T(8,128)S(1)} %cholesky.592), custom_call_target="Cholesky" | custom-call | tf_op jit(solution)/shard_map/jit(cholesky)/cholesky | solution.py:39
  452.3 19.7 %custom-call.80 = f32[2,1,128,128]{2,3,1,0:T(8,128)S(1)} custom-call(f32[2,1,128,128]{3,2,1,0:T(8,128)S(1)} %get-tuple-element.84), custom_call_target="InvertDiagBlocksLowerTriangular" | custom-call | tf_op jit(solution)/shard_map/jit(cholesky)/cholesky | solution.py:39
  473.4 3.8 fusion.31
  477.2 23.5 %custom-call.81 = f32[2,128,128]{2,1,0:T(8,128)S(1)} custom-call(f32[2,128,128]{2,1,0:T(8,128)S(1)} %cholesky.597), custom_call_target="Cholesky" | custom-call | tf_op jit(solution)/shard_map/jit(cholesky)/cholesky | solution.py:39
  501.3 20.1 %custom-call.82 = f32[2,1,128,128]{2,3,1,0:T(8,128)S(1)} custom-call(f32[2,1,128,128]{3,2,1,0:T(8,128)S(1)} %get-tuple-element.82), custom_call_target="InvertDiagBlocksLowerTriangular" | custom-call | tf_op jit(solution)/shard_map/jit(cholesky)/cholesky | solution.py:39
  522.7 3.7 fusion.34
  526.4 23.5 %custom-call.83 = f32[2,128,128]{2,1,0:T(8,128)S(1)} custom-call(f32[2,128,128]{2,1,0:T(8,128)S(1)} %cholesky.602), custom_call_target="Cholesky" | custom-call | tf_op jit(solution)/shard_map/jit(cholesky)/cholesky | solution.py:39
  550.6 19.7 %custom-call.84 = f32[2,1,128,128]{2,3,1,0:T(8,128)S(1)} custom-call(f32[2,1,128,128]{3,2,1,0:T(8,128)S(1)} %get-tuple-element.80), custom_call_target="InvertDiagBlocksLowerTriangular" | custom-call | tf_op jit(solution)/shard_map/jit(cholesky)/cholesky | solution.py:39
  571.4 3.2 fusion.37
  574.6 23.6 %custom-call.85 = f32[2,128,128]{2,1,0:T(8,128)S(1)} custom-call(f32[2,128,128]{2,1,0:T(8,128)S(1)} %cholesky.607), custom_call_target="Cholesky" | custom-call | tf_op jit(solution)/shard_map/jit(cholesky)/cholesky | solution.py:39
  598.9 19.7 %custom-call.86 = f32[2,1,128,128]{2,3,1,0:T(8,128)S(1)} custom-call(f32[2,1,128,128]{3,2,1,0:T(8,128)S(1)} %get-tuple-element.78), custom_call_target="InvertDiagBlocksLowerTriangular" | custom-call | tf_op jit(solution)/shard_map/jit(cholesky)/cholesky | solution.py:39
  619.5 2.6 convolution_subtract_fusion.1
  622.1 23.7 %custom-call.87 = f32[2,128,128]{2,1,0:T(8,128)S(1)} custom-call(f32[2,128,128]{2,1,0:T(8,128)S(1)} %convolution_subtract_fusion.1), custom_call_target="Cholesky" | custom-call | tf_op jit(solution)/shard_map/jit(cholesky)/cholesky | solution.py:39
  647.9 4.7 select_select_fusion
  652.7 4.3 fusion.6
  657.0 22.6 %while.8 = (s32[]{:T(128)}, f32[1024,1024]{1,0:T(8,128)}, s32[8,2]{0,1:T(2,128)S(1)}, f32[8,128,128]{2,1,0:T(8,128)S(1)}, s32[]{:T(128)}) while((s32[]{:T(128)}, f32[1024,1024]{1,0:T(8,128)}, s32[8,2]{0,1:T(2,128)S(1)}, f32[8,128,128]{2,1,0:T(8,128)S(1)}, s32[]{:T(128)}) %tuple.126), condition=%wide.while_cond.1, body=%wide.while_body.1.sunk | while | flops 2 | bytes 131189 | solution.py:10
  657.6 2.2 bitcast_dynamic-update-slice_fusion.4
  660.4 2.2 bitcast_dynamic-update-slice_fusion.4
  663.2 2.2 bitcast_dynamic-update-slice_fusion.4
  679.5 78.6 %custom-call.91 = f32[8,128,128]{1,2,0:T(8,128)S(1)} custom-call(f32[8,128,128]{2,1,0:T(8,128)S(1)} %get-tuple-element.35), custom_call_target="InvertDiagBlocksLowerTriangular" | custom-call | tf_op jit(solution)/shard_map/jit(_solve_triangular)/triangular_solve | solution.py:10
  779.5 4.1 convolution_convert_fusion.1
  783.8 23.6 %while.9 = (s32[]{:T(128)}, f32[1024,1024]{1,0:T(8,128)}, s32[8,2]{0,1:T(2,128)S(1)}, f32[8,128,128]{2,1,0:T(8,128)S(1)}, s32[]{:T(128)}) while((s32[]{:T(128)}, f32[1024,1024]{1,0:T(8,128)}, s32[8,2]{0,1:T(2,128)S(1)}, f32[8,128,128]{2,1,0:T(8,128)S(1)}, s32[]{:T(128)}) %tuple.146), condition=%wide.while_cond.1.clone, body=%wide.while_body.1.clone.sunk | while | flops 2 | bytes 131189 | solution.py:10
  784.4 2.3 bitcast_dynamic-update-slice_fusion.5
  787.4 2.3 bitcast_dynamic-update-slice_fusion.5
  790.3 2.3 bitcast_dynamic-update-slice_fusion.5
  793.3 2.3 bitcast_dynamic-update-slice_fusion.5
  796.3 2.3 bitcast_dynamic-update-slice_fusion.5
  799.2 2.3 bitcast_dynamic-update-slice_fusion.5
  802.2 2.3 bitcast_dynamic-update-slice_fusion.5
  805.1 2.2 bitcast_dynamic-update-slice_fusion.5
  809.0 3.7 fusion.7
  813.0 4.3 fusion.92
  817.3 78.6 %custom-call.93 = f32[8,128,128]{1,2,0:T(8,128)S(1)} custom-call(f32[8,128,128]{2,1,0:T(8,128)S(1)} %get-tuple-element.37), custom_call_target="InvertDiagBlocksLowerTriangular" | custom-call | tf_op jit(solution)/shard_map/jit(_solve_triangular)/triangular_solve | solution.py:10
  895.9 41.9 %all-reduce.9.cloned.1.call-done = f32[32,512]{1,0:T(8,128)} async-done(((f32[32,512]{1,0:T(8,128)}), f32[32,512]{1,0:T(8,128)}) %all-reduce.9.cloned.1.call-update) | async-done | bytes 65552 | tf_op jit(solution)/shard_map/psum | solution.py:47
  962.0 4.1 convolution_convert_fusion
  966.9 21.2 %all-reduce.11.cloned.1.call-done = bf16[32,3904]{1,0:T(8,128)(2,1)} async-done(((bf16[32,3904]{1,0:T(8,128)(2,1)}), bf16[32,3904]{1,0:T(8,128)(2,1)}) %all-reduce.11.cloned.1.call-update) | async-done | bytes 249872 | tf_op jit(solution)/shard_map/psum | solution.py:56
  990.0 179.1 %psum.55 = f32[32]{0:T(128)S(1)} all-reduce(f32[32]{0:T(128)S(1)} %get-tuple-element.65), channel_id=1, replica_groups=mesh['ind'=64,'snp'=2] {'ind'}, use_global_device_ids=true, to_apply=%region_23.27 | all-reduce | flops 32 | bytes 256 | tf_op jit(solution)/shard_map/psum | solution.py:59
  (238 shorter events, 96.5 us)
Async XLA Ops:
  7.2 207.5 %copy-start = (f32[2048]{0:T(1024)S(1)}, f32[2048]{0:T(1024)}, u32[]{:S(2)}) copy-start(f32[2048]{0:T(1024)} %param.18) | copy-start | bytes 24580
  7.2 30.2 %all-gather.11.cloned.1.call-start = ((), (), s32[]{:S(2)}) async-start(), calls=%async_computation.5 | async-start | bytes 11993088 | tf_op jit(solution)/shard_map/all_gather | solution.py:29
  12.8 1.0 copy-start.6
  12.8 49.6 %all-gather.13.cloned.1.call-start = ((), (), s32[]{:S(2)}) async-start(), calls=%async_computation.6 | async-start | bytes 11993088 | tf_op jit(solution)/shard_map/all_gather | solution.py:29
  13.5 200.4 %all-reduce.13.cloned.1.call-start = ((), (), s32[]{:S(2)}) async-start(), calls=%async_computation.7 | async-start | bytes 8519680 | tf_op jit(solution)/shard_map/psum | solution.py:34
  72.7 142.0 %copy-start.12 = (f32[32]{0:T(128)S(1)}, f32[32]{0:T(128)}, u32[]{:S(2)}) copy-start(f32[32]{0:T(128)} %param.20) | copy-start | bytes 388
  72.7 142.0 %copy-start.11 = (s32[2048]{0:T(1024)S(1)}, s32[2048]{0:T(1024)}, u32[]{:S(2)}) copy-start(s32[2048]{0:T(1024)} %param.19) | copy-start | bytes 24580
  72.7 157.4 %all-gather.7.cloned.1.call-start = ((), (), s32[]{:S(2)}) async-start(), calls=%async_computation | async-start | bytes 6291456 | tf_op jit(solution)/shard_map/all_gather | solution.py:35
  214.0 35.0 %all-gather.9.cloned.1.call-start = ((), (), s32[]{:S(2)}) async-start(), calls=%async_computation.1 | async-start | bytes 6291456 | tf_op jit(solution)/shard_map/all_gather | solution.py:35
  214.6 594.4 %all-reduce.7.cloned.1.call-start = ((), (), s32[]{:S(2)}) async-start(), calls=%async_computation.2 | async-start | bytes 507904 | tf_op jit(solution)/shard_map/psum | solution.py:56
  214.7 12.3 %copy-start.9 = (f32[2,32,512]{2,1,0:T(8,128)S(1)}, f32[2,32,512]{2,1,0:T(8,128)}, u32[]{:S(2)}) copy-start(f32[2,32,512]{2,1,0:T(8,128)} %param.16) | copy-start | bytes 393220
  227.0 7.6 copy-start.10
  230.1 6.7 copy-start.5
  249.0 4.7 copy-start.2
  251.7 2.0 copy-start.3
  273.4 3.2 copy-start.4
  656.9 111.9 %copy-start.8 = (f32[2,32,1024]{2,1,0:T(8,128)S(1)}, f32[2,32,1024]{2,1,0:T(8,128)}, u32[]{:S(2)}) copy-start(f32[2,32,1024]{2,1,0:T(8,128)} %param.17) | copy-start | bytes 786436
  783.7 154.2 %all-reduce.9.cloned.1.call-start = ((), (), s32[]{:S(2)}) async-start(), calls=%async_computation.3 | async-start | bytes 131072 | tf_op jit(solution)/shard_map/psum | solution.py:47
  812.7 175.3 %all-reduce.11.cloned.1.call-start = ((), (), s32[]{:S(2)}) async-start(), calls=%async_computation.4 | async-start | bytes 507904 | tf_op jit(solution)/shard_map/psum | solution.py:56
  955.4 32.6 %copy-start.7 = (bf16[32,3904]{1,0:T(8,128)(2,1)S(1)}, bf16[32,3904]{1,0:T(8,128)(2,1)}, u32[]{:S(2)}) copy-start(bf16[32,3904]{1,0:T(8,128)(2,1)} %all-reduce.7.cloned.1.call-done) | copy-start | bytes 749572
  958.6 210.9 %copy-start.1 = (f32[2048]{0:T(1024)S(1)}, f32[2048]{0:T(1024)}, u32[]{:S(2)}) copy-start(f32[2048]{0:T(1024)} %param.18) | copy-start | bytes 24580
  958.7 210.3 %copy-start.13 = (f32[32]{0:T(128)S(1)}, f32[32]{0:T(128)}, u32[]{:S(2)}) copy-start(f32[32]{0:T(128)} %param.21) | copy-start | bytes 388
Sparse Core Ops, SparseCore 0:
  12.9 24.3 all-gather.10
  39.0 23.3 all-gather.12
  72.8 141.0 all-reduce.12
  215.6 14.1 all-gather.6
  231.3 17.6 all-gather.8
  783.8 25.1 all-reduce.6
  814.2 123.5 all-reduce.8
  966.3 21.6 all-reduce.10
where the time goes:
time: 1190 us; the launch traced here: 1180 us
  other arithmetic  520 us (44%)
  waiting for transfers between devices  252 us (21%)
  blocking collectives  185 us (16%)
  matrix products  120 us (10%)
  local copies, waits for them, and re-layouts  82.7 us (7%)
  between operations  15.9 us (1%)
    another operation x33, other arithmetic, local(): factors = jnp.linalg.cholesky(jnp.stack(shifted))  343 us
    psum x1, blocking collectives, local(): squares_sum = lax.psum(jnp.sum(residual * residual, axis=1), 'ind')  179 us
    another operation x5, other arithmetic, sample_effects(): jax.scipy.linalg.solve_triangular(factor, moved, lower=True, trans=1)  162 us
    psum x1, waiting for transfers between devices, local(): summed_gram = lax.psum(partial_gram, 'ind')  141 us
    another operation x59, local copies, waits for them, and re-layouts, sample_effects(): jax.scipy.linalg.solve_triangular(factor, moved, lower=True, trans=1)  45.9 us
    psum x1, waiting for transfers between devices, local(): summed_scores = lax.psum(local_scores, 'ind')  41.9 us
    all_gather x2, waiting for transfers between devices, local(): lax.all_gather(genotype_block, 'snp', axis=1, tiled=True)  34.7 us
    another operation x14, matrix products, local(): factors = jnp.linalg.cholesky(jnp.stack(shifted))  33.6 us
  transfers between devices with their start and end apart: 8, of which 7 were waited for; matrix products, arithmetic and copies ran while one was open for 12% of the time, Pallas kernels for 0%

commit v1 on v0

--- a/solution.py
+++ b/solution.py
@@ -44,7 +44,7 @@
         rounded = residual.astype(jnp.bfloat16)
         carried = jnp.dot(previous, gram_matrix, precision=lax.Precision.HIGHEST)
         local_scores = jnp.dot(rounded, genotypes[block_index], preferred_element_type=jnp.float32)
-        summed_scores = lax.psum(local_scores, "ind")
+        summed_scores = jnp.sum(lax.all_gather(local_scores, "ind"), axis=0)
         own_half = summed_scores + lax.dynamic_slice_in_dim(carried, own_offset, half_width, 1)
         right_side = lax.all_gather(own_half, "snp", axis=1, tiled=True)
         sampled = sample_effects(factors[block_index], right_side, noise[block_index], chain_scale)

time: 1190 us -> 1240 us (1.042)
  waiting for transfers between devices: 252 us -> 303 us
    all_gather x0 -> x2, waiting for transfers between devices: none -> 54.1 us  [local(): summed_scores = jnp.sum(lax.all_gather(local_scores, 'ind'), axis=0)]
    psum x1 -> x0, waiting for transfers between devices: 41.9 us -> none  [local(): summed_scores = lax.psum(local_scores, 'ind')]
    psum x2, waiting for transfers between devices: 22.8 us -> 49.9 us  [local(): lax.psum(partial_update.astype(jnp.bfloat16), 'snp').astype(jnp.float32)]
    all_gather x2, waiting for transfers between devices: 9.9 us -> 23.5 us  [local(): gram_matrix = lax.all_gather(summed_gram, 'snp', axis=1, tiled=True)]
  transfers between devices with their start and end apart: 8 -> 9, of which waited for: 7 -> 8; matrix products, arithmetic and copies ran while one was open for 12% -> 12% of each run, Pallas kernels for 0% -> 0%
where the time goes in v1:
time: 1240 us; the launch traced here: 1230 us
  other arithmetic  525 us (42%)
  waiting for transfers between devices  303 us (24%)
  blocking collectives  185 us (15%)
  matrix products  120 us (10%)
  local copies, waits for them, and re-layouts  83.8 us (7%)
  between operations  15.6 us (1%)
    another operation x33, other arithmetic, local(): factors = jnp.linalg.cholesky(jnp.stack(shifted))  343 us
    psum x1, blocking collectives, local(): squares_sum = lax.psum(jnp.sum(residual * residual, axis=1), 'ind')  179 us
    another operation x5, other arithmetic, sample_effects(): jax.scipy.linalg.solve_triangular(factor, moved, lower=True, trans=1)  162 us
    psum x1, waiting for transfers between devices, local(): summed_gram = lax.psum(partial_gram, 'ind')  136 us
    all_gather x2, waiting for transfers between devices, local(): summed_scores = jnp.sum(lax.all_gather(local_scores, 'ind'), axis=0)  54.1 us
    psum x2, waiting for transfers between devices, local(): lax.psum(partial_update.astype(jnp.bfloat16), 'snp').astype(jnp.float32)  49.9 us
    another operation x59, local copies, waits for them, and re-layouts, sample_effects(): jax.scipy.linalg.solve_triangular(factor, moved, lower=True, trans=1)  46.3 us
    all_gather x2, waiting for transfers between devices, local(): lax.all_gather(genotype_block, 'snp', axis=1, tiled=True)  38.5 us
  transfers between devices with their start and end apart: 9, of which 8 were waited for; matrix products, arithmetic and copies ran while one was open for 12% of the time, Pallas kernels for 0%

profile of v1, /device:TPU:0, one launch (start us, length us, event | category | flops | bytes accessed | tf_op | source)
XLA Modules:
  0.0 1232.9 jit_solution(6301273002744230709)
XLA Ops:
  7.2 5.5 fusion.215
  13.6 23.8 %all-gather.15.cloned.1.call-done = bf16[1,3904,1024]{2,1,0:T(8,128)(2,1)} async-done(((bf16[1,3904,512]{2,1,0:T(8,128)(2,1)}), bf16[1,3904,1024]{2,1,0:T(8,128)(2,1)}) %all-gather.15.cloned.1.call-update) | async-done | bytes 7995408 | tf_op jit(solution)/shard_map/all_gather | solution.py:29
  37.3 10.3 fusion.3
  47.6 14.7 %all-gather.17.cloned.1.call-done = bf16[1,3904,1024]{2,1,0:T(8,128)(2,1)} async-done(((bf16[1,3904,512]{2,1,0:T(8,128)(2,1)}), bf16[1,3904,1024]{2,1,0:T(8,128)(2,1)}) %all-gather.17.cloned.1.call-update) | async-done | bytes 7995408 | tf_op jit(solution)/shard_map/all_gather | solution.py:29
  62.3 10.3 fusion.1
  73.6 3.6 fusion.11
  77.3 135.8 %all-reduce.10.cloned.1.call-done = (f32[1024,512]{0,1:T(8,128)}, f32[1024,512]{0,1:T(8,128)}) async-done(((f32[1024,512]{0,1:T(8,128)}, f32[1024,512]{0,1:T(8,128)}), (f32[1024,512]{0,1:T(8,128)}, f32[1024,512]{0,1:T(8,128)})) %all-reduce.10.cloned.1.call-update) | async-done | bytes 4194320 | tf_op jit(solution)/shard_map/psum | solution.py:34
  213.7 6.2 gather_fusion
  219.9 6.2 gather_fusion.1
  229.2 54.1 %all-gather.19.cloned.1.call-done = f32[2048,512]{1,0:T(8,128)} async-done(((f32[32,512]{1,0:T(8,128)}), f32[2048,512]{1,0:T(8,128)}) %all-gather.19.cloned.1.call-update) | async-done | bytes 4194320 | tf_op jit(solution)/shard_map/all_gather | solution.py:47
  283.3 2.5 reduce_sum.27
  285.8 12.9 %all-gather.11.cloned.1.call-done = f32[1024,1024]{0,1:T(8,128)} async-done(((f32[1024,512]{0,1:T(8,128)}), f32[1024,1024]{0,1:T(8,128)}) %all-gather.11.cloned.1.call-update) | async-done | bytes 4194320 | tf_op jit(solution)/shard_map/all_gather | solution.py:35
  298.7 4.5 fusion.96
  305.2 2.3 add_bitcast_fusion.1
  307.5 10.6 all-gather.13.cloned.1.call-done
  318.1 2.7 add_bitcast_fusion
  322.8 4.1 pad_maximum_fusion
  326.9 8.7 copy.47
  335.6 6.9 fusion
  342.5 3.2 copy-done.4
  345.7 23.5 %custom-call.73 = f32[2,128,128]{2,1,0:T(8,128)S(1)} custom-call(f32[2,128,128]{2,1,0:T(8,128)S(1)} %cholesky.578), custom_call_target="Cholesky" | custom-call | tf_op jit(solution)/shard_map/jit(cholesky)/cholesky | solution.py:39
  369.2 19.7 %custom-call.74 = f32[2,1,128,128]{2,3,1,0:T(8,128)S(1)} custom-call(f32[2,1,128,128]{3,2,1,0:T(8,128)S(1)} %select_bitcast_fusion.6), custom_call_target="InvertDiagBlocksLowerTriangular" | custom-call | tf_op jit(solution)/shard_map/jit(cholesky)/cholesky | solution.py:39
  388.9 4.3 cholesky.253
  393.2 3.1 constant_dynamic-update-slice_fusion.107
  398.4 23.9 %custom-call.75 = f32[2,128,128]{2,1,0:T(8,128)S(1)} custom-call(f32[2,128,128]{2,1,0:T(8,128)S(1)} %cholesky.582), custom_call_target="Cholesky" | custom-call | tf_op jit(solution)/shard_map/jit(cholesky)/cholesky | solution.py:39
  423.0 19.7 %custom-call.76 = f32[2,1,128,128]{2,3,1,0:T(8,128)S(1)} custom-call(f32[2,1,128,128]{3,2,1,0:T(8,128)S(1)} %get-tuple-element.87), custom_call_target="InvertDiagBlocksLowerTriangular" | custom-call | tf_op jit(solution)/shard_map/jit(cholesky)/cholesky | solution.py:39
  444.4 3.2 fusion.25
  447.6 23.6 %custom-call.77 = f32[2,128,128]{2,1,0:T(8,128)S(1)} custom-call(f32[2,128,128]{2,1,0:T(8,128)S(1)} %cholesky.587), custom_call_target="Cholesky" | custom-call | tf_op jit(solution)/shard_map/jit(cholesky)/cholesky | solution.py:39
  472.0 19.7 %custom-call.78 = f32[2,1,128,128]{2,3,1,0:T(8,128)S(1)} custom-call(f32[2,1,128,128]{3,2,1,0:T(8,128)S(1)} %get-tuple-element.85), custom_call_target="InvertDiagBlocksLowerTriangular" | custom-call | tf_op jit(solution)/shard_map/jit(cholesky)/cholesky | solution.py:39
  493.3 3.8 fusion.28
  497.1 23.7 %custom-call.79 = f32[2,128,128]{2,1,0:T(8,128)S(1)} custom-call(f32[2,128,128]{2,1,0:T(8,128)S(1)} %cholesky.592), custom_call_target="Cholesky" | custom-call | tf_op jit(solution)/shard_map/jit(cholesky)/cholesky | solution.py:39
  521.4 19.7 %custom-call.80 = f32[2,1,128,128]{2,3,1,0:T(8,128)S(1)} custom-call(f32[2,1,128,128]{3,2,1,0:T(8,128)S(1)} %get-tuple-element.83), custom_call_target="InvertDiagBlocksLowerTriangular" | custom-call | tf_op jit(solution)/shard_map/jit(cholesky)/cholesky | solution.py:39
  542.6 3.8 fusion.31
  546.4 23.5 %custom-call.81 = f32[2,128,128]{2,1,0:T(8,128)S(1)} custom-call(f32[2,128,128]{2,1,0:T(8,128)S(1)} %cholesky.597), custom_call_target="Cholesky" | custom-call | tf_op jit(solution)/shard_map/jit(cholesky)/cholesky | solution.py:39
  570.5 20.1 %custom-call.82 = f32[2,1,128,128]{2,3,1,0:T(8,128)S(1)} custom-call(f32[2,1,128,128]{3,2,1,0:T(8,128)S(1)} %get-tuple-element.81), custom_call_target="InvertDiagBlocksLowerTriangular" | custom-call | tf_op jit(solution)/shard_map/jit(cholesky)/cholesky | solution.py:39
  591.9 3.7 fusion.34
  595.6 23.5 %custom-call.83 = f32[2,128,128]{2,1,0:T(8,128)S(1)} custom-call(f32[2,128,128]{2,1,0:T(8,128)S(1)} %cholesky.602), custom_call_target="Cholesky" | custom-call | tf_op jit(solution)/shard_map/jit(cholesky)/cholesky | solution.py:39
  619.7 19.7 %custom-call.84 = f32[2,1,128,128]{2,3,1,0:T(8,128)S(1)} custom-call(f32[2,1,128,128]{3,2,1,0:T(8,128)S(1)} %get-tuple-element.79), custom_call_target="InvertDiagBlocksLowerTriangular" | custom-call | tf_op jit(solution)/shard_map/jit(cholesky)/cholesky | solution.py:39
  640.5 3.2 fusion.37
  643.7 23.6 %custom-call.85 = f32[2,128,128]{2,1,0:T(8,128)S(1)} custom-call(f32[2,128,128]{2,1,0:T(8,128)S(1)} %cholesky.607), custom_call_target="Cholesky" | custom-call | tf_op jit(solution)/shard_map/jit(cholesky)/cholesky | solution.py:39
  668.1 19.7 %custom-call.86 = f32[2,1,128,128]{2,3,1,0:T(8,128)S(1)} custom-call(f32[2,1,128,128]{3,2,1,0:T(8,128)S(1)} %get-tuple-element.77), custom_call_target="InvertDiagBlocksLowerTriangular" | custom-call | tf_op jit(solution)/shard_map/jit(cholesky)/cholesky | solution.py:39
  688.7 2.6 convolution_subtract_fusion.1
  691.3 23.7 %custom-call.87 = f32[2,128,128]{2,1,0:T(8,128)S(1)} custom-call(f32[2,128,128]{2,1,0:T(8,128)S(1)} %convolution_subtract_fusion.1), custom_call_target="Cholesky" | custom-call | tf_op jit(solution)/shard_map/jit(cholesky)/cholesky | solution.py:39
  717.1 4.7 select_select_fusion
  721.8 4.2 fusion.6
  726.1 23.2 %while.8 = (s32[]{:T(128)}, f32[1024,1024]{1,0:T(8,128)}, s32[8,2]{0,1:T(2,128)S(1)}, f32[8,128,128]{2,1,0:T(8,128)S(1)}, s32[]{:T(128)}) while((s32[]{:T(128)}, f32[1024,1024]{1,0:T(8,128)}, s32[8,2]{0,1:T(2,128)S(1)}, f32[8,128,128]{2,1,0:T(8,128)S(1)}, s32[]{:T(128)}) %tuple.126), condition=%wide.while_cond.1, body=%wide.while_body.1.sunk | while | flops 2 | bytes 131189 | solution.py:10
  726.7 2.3 bitcast_dynamic-update-slice_fusion.4
  729.6 2.3 bitcast_dynamic-update-slice_fusion.4
  732.5 2.3 bitcast_dynamic-update-slice_fusion.4
  735.4 2.3 bitcast_dynamic-update-slice_fusion.4
  738.3 2.3 bitcast_dynamic-update-slice_fusion.4
  741.2 2.3 bitcast_dynamic-update-slice_fusion.4
  744.2 2.3 bitcast_dynamic-update-slice_fusion.4
  749.3 78.6 %custom-call.91 = f32[8,128,128]{1,2,0:T(8,128)S(1)} custom-call(f32[8,128,128]{2,1,0:T(8,128)S(1)} %get-tuple-element.35), custom_call_target="InvertDiagBlocksLowerTriangular" | custom-call | tf_op jit(solution)/shard_map/jit(_solve_triangular)/triangular_solve | solution.py:10
  849.3 4.1 convolution_convert_fusion.1
  853.5 25.3 %all-reduce.6.cloned.1.call-done = bf16[32,3904]{1,0:T(8,128)(2,1)} async-done(((bf16[32,3904]{1,0:T(8,128)(2,1)}), bf16[32,3904]{1,0:T(8,128)(2,1)}) %all-reduce.6.cloned.1.call-update) | async-done | bytes 249872 | tf_op jit(solution)/shard_map/psum | solution.py:56
  878.8 3.7 fusion.7
  882.5 23.6 %while.9 = (s32[]{:T(128)}, f32[1024,1024]{1,0:T(8,128)}, s32[8,2]{0,1:T(2,128)S(1)}, f32[8,128,128]{2,1,0:T(8,128)S(1)}, s32[]{:T(128)}) while((s32[]{:T(128)}, f32[1024,1024]{1,0:T(8,128)}, s32[8,2]{0,1:T(2,128)S(1)}, f32[8,128,128]{2,1,0:T(8,128)S(1)}, s32[]{:T(128)}) %tuple.148), condition=%wide.while_cond.1.clone, body=%wide.while_body.1.clone.sunk | while | flops 2 | bytes 131189 | solution.py:10
  906.1 78.6 %custom-call.93 = f32[8,128,128]{1,2,0:T(8,128)S(1)} custom-call(f32[8,128,128]{2,1,0:T(8,128)S(1)} %get-tuple-element.37), custom_call_target="InvertDiagBlocksLowerTriangular" | custom-call | tf_op jit(solution)/shard_map/jit(_solve_triangular)/triangular_solve | solution.py:10
  984.7 4.3 fusion.92
  989.1 2.5 reduce_sum.28
  1015.0 4.1 convolution_convert_fusion
  1019.8 24.6 %all-reduce.8.cloned.1.call-done = bf16[32,3904]{1,0:T(8,128)(2,1)} async-done(((bf16[32,3904]{1,0:T(8,128)(2,1)}), bf16[32,3904]{1,0:T(8,128)(2,1)}) %all-reduce.8.cloned.1.call-update) | async-done | bytes 249872 | tf_op jit(solution)/shard_map/psum | solution.py:56
  1046.3 179.1 %psum.39 = f32[32]{0:T(128)S(1)} all-reduce(f32[32]{0:T(128)S(1)} %get-tuple-element.64), channel_id=1, replica_groups=mesh['ind'=64,'snp'=2] {'ind'}, use_global_device_ids=true, to_apply=%region_23.27 | all-reduce | flops 32 | bytes 256 | tf_op jit(solution)/shard_map/psum | solution.py:59
  (241 shorter events, 103.8 us)
Async XLA Ops:
  7.2 206.6 %copy-start = (f32[2048]{0:T(1024)S(1)}, f32[2048]{0:T(1024)}, u32[]{:S(2)}) copy-start(f32[2048]{0:T(1024)} %param.18) | copy-start | bytes 24580
  7.2 30.1 %all-gather.15.cloned.1.call-start = ((), (), s32[]{:S(2)}) async-start(), calls=%async_computation.4 | async-start | bytes 11993088 | tf_op jit(solution)/shard_map/all_gather | solution.py:29
  12.8 49.6 %all-gather.17.cloned.1.call-start = ((), (), s32[]{:S(2)}) async-start(), calls=%async_computation.5 | async-start | bytes 11993088 | tf_op jit(solution)/shard_map/all_gather | solution.py:29
  13.5 199.5 %all-reduce.10.cloned.1.call-start = ((), (), s32[]{:S(2)}) async-start(), calls=%async_computation.8 | async-start | bytes 8388608 | tf_op jit(solution)/shard_map/psum | solution.py:34
  72.6 1.0 copy-start.6
  72.6 141.1 %copy-start.11 = (f32[32]{0:T(128)S(1)}, f32[32]{0:T(128)}, u32[]{:S(2)}) copy-start(f32[32]{0:T(128)} %param.20) | copy-start | bytes 388
  72.6 141.1 %copy-start.10 = (s32[2048]{0:T(1024)S(1)}, s32[2048]{0:T(1024)}, u32[]{:S(2)}) copy-start(s32[2048]{0:T(1024)} %param.19) | copy-start | bytes 24580
  72.6 210.7 %all-gather.19.cloned.1.call-start = ((), (), s32[]{:S(2)}) async-start(), calls=%async_computation.6 | async-start | bytes 4259840 | tf_op jit(solution)/shard_map/all_gather | solution.py:47
  77.2 221.5 %all-gather.11.cloned.1.call-start = ((), (), s32[]{:S(2)}) async-start(), calls=%async_computation | async-start | bytes 6291456 | tf_op jit(solution)/shard_map/all_gather | solution.py:35
  213.0 105.0 %all-gather.13.cloned.1.call-start = ((), (), s32[]{:S(2)}) async-start(), calls=%async_computation.1 | async-start | bytes 6291456 | tf_op jit(solution)/shard_map/all_gather | solution.py:35
  213.6 665.1 %all-reduce.6.cloned.1.call-start = ((), (), s32[]{:S(2)}) async-start(), calls=%async_computation.2 | async-start | bytes 507904 | tf_op jit(solution)/shard_map/psum | solution.py:56
  213.7 12.3 %copy-start.9 = (f32[2,32,512]{2,1,0:T(8,128)S(1)}, f32[2,32,512]{2,1,0:T(8,128)}, u32[]{:S(2)}) copy-start(f32[2,32,512]{2,1,0:T(8,128)} %param.16) | copy-start | bytes 393220
  298.7 6.4 copy-start.5
  318.1 4.7 copy-start.2
  320.8 2.0 copy-start.3
  342.5 3.2 copy-start.4
  726.1 112.6 %copy-start.8 = (f32[2,32,1024]{2,1,0:T(8,128)S(1)}, f32[2,32,1024]{2,1,0:T(8,128)}, u32[]{:S(2)}) copy-start(f32[2,32,1024]{2,1,0:T(8,128)} %param.17) | copy-start | bytes 786436
  853.4 135.6 %all-gather.21.cloned.1.call-start = ((), (), s32[]{:S(2)}) async-start(), calls=%async_computation.7 | async-start | bytes 4259840 | tf_op jit(solution)/shard_map/all_gather | solution.py:47
  882.4 162.0 %all-reduce.8.cloned.1.call-start = ((), (), s32[]{:S(2)}) async-start(), calls=%async_computation.3 | async-start | bytes 507904 | tf_op jit(solution)/shard_map/psum | solution.py:56
  1008.3 36.1 %copy-start.7 = (bf16[32,3904]{1,0:T(8,128)(2,1)S(1)}, bf16[32,3904]{1,0:T(8,128)(2,1)}, u32[]{:S(2)}) copy-start(bf16[32,3904]{1,0:T(8,128)(2,1)} %all-reduce.6.cloned.1.call-done) | copy-start | bytes 749572
  1011.6 214.3 %copy-start.1 = (f32[2048]{0:T(1024)S(1)}, f32[2048]{0:T(1024)}, u32[]{:S(2)}) copy-start(f32[2048]{0:T(1024)} %param.18) | copy-start | bytes 24580
  1011.6 213.8 %copy-start.12 = (f32[32]{0:T(128)S(1)}, f32[32]{0:T(128)}, u32[]{:S(2)}) copy-start(f32[32]{0:T(128)} %param.21) | copy-start | bytes 388
Sparse Core Ops, SparseCore 0:
  12.9 24.3 all-gather.14
  39.0 23.3 all-gather.16
  72.7 140.2 all-reduce.9
  216.7 66.5 all-gather.18
  284.9 13.7 all-gather.10
  300.3 17.6 all-gather.12
  853.6 25.1 all-reduce.5
  882.6 70.7 all-gather.20
  1019.2 25.1 all-reduce.7
